TPU v7x, 512 devices: a whole 4x4x16 slice. The times are simulated.
512 devices in a mesh: rows: 128 (over z, y, core), rep: 4 (over x).
Axes of the slice: x: 4, y: 4, z: 16, core: 2. Of those that a mesh axis runs over, the one named last changes fastest.
Arguments:
- embeddings: bfloat16 [65536, 1024], P(('rows', 'rep')), may hold values from -6 to 6
- parent_id: int32 [65536], P(('rows', 'rep')), may hold values from 0 to 1023
- send_list: int32 [512, 128, 2], P(('rows', 'rep')), may hold values from 0 to 127, as said below
- send_count: int32 [512, 128], P(('rows', 'rep')), may hold values from 0 to 2, as said below
- child_count: int32 [1024], P('rows'), may hold values from 64 to 128, as said below
- centroids: bfloat16 [1024, 128, 1024], P('rows'), may hold values from -24 to 24
Outputs:
- updated_centroids: float32 [1024, 128, 1024], P('rows', 'rep')
- row_energy: float32 [65536], P(('rows', 'rep'))
Inputs may be any that keep to these rules, and one draw needn't show every extreme that they name: For device d and owner o, the first send_count[d, o] entries of send_list[d, o] name distinct local rows whose parent_id // 8 == o; every local row of d is named exactly once over all owners; entries past the count are 0. `send_count`: each device's counts sum to 128; one owner, the same for every device, gets exactly 2 rows from every device. `child_count`: some parent has 128 live children.
All inputs are finite; a program needn't handle non-finite values.
Results may differ from a plain program's by a relative error of at most 0.0038.
Values may be sent and summed in bfloat16 or wider, within the bound.
A program may use at most 64 MiB of HBM per device.

v0:
```python
import jax
import jax.numpy as jnp
from jax import lax
from jax.sharding import PartitionSpec as P

ITERS = 2


inverse_temp = 1.0 / 32.0
prior_weight = 1.0


def block_terms(row_block, sub_rows, live_rows, child_panel, child_count):
    par_dev, kids, width = child_panel.shape
    flat_kids = child_panel.reshape(par_dev * kids, width)
    raw_affinities = jnp.dot(row_block, flat_kids.T, preferred_element_type=jnp.float32)
    kid_norms = jnp.sum(jnp.square(flat_kids.astype(jnp.float32)), axis=1)
    column = jnp.arange(par_dev * kids, dtype=jnp.int32)
    column_parent = column // kids
    column_open = column % kids < jnp.repeat(child_count, kids)
    allowed = (column_parent[None, :] == sub_rows[:, None]) & column_open[None, :]
    logits = jnp.where(
        allowed, (2.0 * raw_affinities - kid_norms[None, :]) * inverse_temp, -jnp.inf
    )
    row_top = jnp.max(logits, axis=1)
    exp_terms = jnp.where(allowed, jnp.exp(logits - row_top[:, None]), 0.0)
    exp_total = jnp.sum(exp_terms, axis=1)
    energy = row_top + jnp.log(exp_total)
    weights_full = exp_terms / exp_total[:, None] * live_rows[:, None]
    weights_half = weights_full.astype(jnp.bfloat16)
    sum_rows = jnp.dot(weights_half.T, row_block, preferred_element_type=jnp.float32)
    return (sum_rows, jnp.sum(weights_full, axis=0), energy)


def evaluate(received, child_panel, child_count):
    arrived, arrived_sub, arrived_count = received
    senders, slot_width, width = arrived.shape
    position_overall_sum = senders * slot_width
    block_rows = min(512, position_overall_sum)
    flat_rows = arrived.reshape(position_overall_sum, width)
    flat_sub = arrived_sub.reshape(position_overall_sum)
    live_slot = lax.broadcasted_iota(jnp.int32, (senders, slot_width), 1) < arrived_count[:, None]
    columns = child_panel.shape[0] * child_panel.shape[1]
    live_used = live_slot.reshape(position_overall_sum).astype(jnp.float32)
    block_count = position_overall_sum // block_rows

    def visit(block_index, state_now):
        sum_acc, weight_acc, energy_acc = state_now
        sum_rows, weight_rows, energy = block_terms(
            flat_rows, flat_sub, live_used, child_panel, child_count
        )
        return (sum_acc + sum_rows, weight_acc + weight_rows, energy)

    initial = (
        jnp.zeros((columns, width), jnp.float32),
        jnp.zeros((columns,), jnp.float32),
        jnp.zeros((position_overall_sum,), jnp.float32),
    )
    sum_acc, weight_acc, energy_acc = lax.fori_loop(0, block_count, visit, initial)
    energy_slots = energy_acc.reshape(senders, slot_width)
    return (sum_acc, weight_acc, energy_slots)


def on_device(embeddings, parent_id, send_list, send_count, child_count, centroids):
    listing = send_list[0]
    counting = send_count[0]
    owners, slot_width = listing.shape
    par_dev, kids, width = centroids.shape
    rep_count = lax.axis_size("rep")
    share_kids = kids // rep_count
    rep_index = lax.axis_index("rep")
    filled = lax.broadcasted_iota(jnp.int32, (owners, slot_width), 1) < counting[:, None]
    outgoing = embeddings[listing]
    sub_parent = parent_id[listing] % par_dev

    def deliver():
        return (
            lax.all_to_all(outgoing, "rows", split_axis=0, concat_axis=0, tiled=True),
            lax.all_to_all(sub_parent, "rows", split_axis=0, concat_axis=0, tiled=True),
            lax.all_to_all(counting, "rows", split_axis=0, concat_axis=0, tiled=True),
        )

    child_panel = centroids
    received = deliver()
    for iteration in range(ITERS):
        if iteration > 0:
            received = deliver()
        sum_acc, weight_acc, energy_slots = evaluate(received, child_panel, child_count)
        sum_acc = sum_acc.reshape(par_dev, kids, width)
        weight_acc = weight_acc.reshape(par_dev, kids)
        part_sums = lax.psum_scatter(
            sum_acc.astype(jnp.bfloat16), "rep", scatter_dimension=1, tiled=True
        ).astype(jnp.float32)
        full_weights = lax.psum(weight_acc, "rep")
        part_weights = lax.dynamic_slice_in_dim(full_weights, rep_index * share_kids, share_kids, 1)
        old_part = lax.dynamic_slice_in_dim(
            child_panel, rep_index * share_kids, share_kids, 1
        ).astype(jnp.float32)
        updated = (part_sums + prior_weight * old_part) / (part_weights[:, :, None] + prior_weight)
        if iteration + 1 < ITERS:
            child_panel = lax.all_gather(updated.astype(jnp.bfloat16), "rep", axis=1, tiled=True)
    returned = lax.all_to_all(energy_slots, "rows", split_axis=0, concat_axis=0, tiled=True)
    contributions = jnp.where(filled, returned, 0.0)
    row_energy = (
        jnp.zeros((embeddings.shape[0],), jnp.float32)
        .at[listing.reshape(-1)]
        .add(contributions.reshape(-1))
    )
    return (updated, row_energy)


def solution(mesh):
    in_specs = (
        P(("rows", "rep"), None),
        P(("rows", "rep")),
        P(("rows", "rep"), None, None),
        P(("rows", "rep"), None),
        P("rows"),
        P("rows", None, None),
    )
    out_specs = (P("rows", "rep", None), P(("rows", "rep")))
    return jax.shard_map(
        on_device, mesh=mesh, in_specs=in_specs, out_specs=out_specs, check_vma=False
    )
```

profile of v0, /device:TPU:1, one launch (start us, length us, event | category | flops | bytes accessed | tf_op | source)
XLA Modules:
  0.0 233.4 jit_solution(13153984374085480395)
XLA Ops:
  7.2 1.4 copy.23
  8.6 20.6 %all-to-all-start.2 = ((s32[128,1,1]{2,1,0:T(1,128)}), s32[128,1,1]{2,1,0:T(1,128)S(1)}, u32[]{:S(2)}, u32[]{:S(2)}) async-start(s32[128,1,1]{2,1,0:T(1,128)} %copy.23), calls=%async_computation.2 | async-start | bytes 131072 | tf_op jit(solution)/shard_map/all_to_all | solution.py:80
  30.2 1.9 gather_fusion
  32.8 11.2 %all-to-all-done.2 = s32[128,1,1]{2,1,0:T(1,128)S(1)} async-done(((s32[128,1,1]{2,1,0:T(1,128)}), s32[128,1,1]{2,1,0:T(1,128)S(1)}, u32[]{:S(2)}, u32[]{:S(2)}) %all-to-all-start.2) | async-done | bytes 544 | tf_op jit(solution)/shard_map/all_to_all | solution.py:80
  44.0 5.7 %all-to-all-start = ((s32[128,1,2]{2,1,0:T(1,128)}), s32[128,1,2]{2,1,0:T(1,128)S(1)}, u32[]{:S(2)}, u32[]{:S(2)}) async-start(s32[128,1,2]{2,1,0:T(1,128)} %bitcast.1), calls=%async_computation | async-start | bytes 131072 | tf_op jit(solution)/shard_map/all_to_all | solution.py:79
  49.7 1.2 gather_fusion.1
  51.9 12.8 %all-to-all-done = s32[128,1,2]{2,1,0:T(1,128)S(1)} async-done(((s32[128,1,2]{2,1,0:T(1,128)}), s32[128,1,2]{2,1,0:T(1,128)S(1)}, u32[]{:S(2)}, u32[]{:S(2)}) %all-to-all-start) | async-done | bytes 1056 | tf_op jit(solution)/shard_map/all_to_all | solution.py:79
  64.7 5.7 %all-to-all-start.1 = ((bf16[128,2,1024]{2,1,0:T(2,128)(2,1)}), bf16[128,2,1024]{2,1,0:T(2,128)(2,1)S(1)}, u32[]{:S(2)}, u32[]{:S(2)}) async-start(bf16[128,2,1024]{2,1,0:T(2,128)(2,1)} %reshape.241), calls=%async_computation.1 | async-start | bytes 1048576 | tf_op jit(solution)/shard_map/all_to_all | solution.py:78
  70.6 2.1 multiply_reduce_fusion.1
  72.7 2.4 %reduce.3 = s32[128]{0:T(128)S(1)} reduce(s32[128,1,1]{2,1,0:T(1,128)S(1)} %all-to-all-done.2, s32[]{:T(128)} %constant.87.clone.1), dimensions={1,2}, to_apply=%all_to_all.25.reduce_sub_computation | reduce | bytes 1028 | tf_op jit(solution)/shard_map/all_to_all | solution.py:80
  76.8 24.8 %all-to-all-done.1 = bf16[128,2,1024]{2,1,0:T(2,128)(2,1)S(1)} async-done(((bf16[128,2,1024]{2,1,0:T(2,128)(2,1)}), bf16[128,2,1024]{2,1,0:T(2,128)(2,1)S(1)}, u32[]{:S(2)}, u32[]{:S(2)}) %all-to-all-start.1) | async-done | bytes 524320 | tf_op jit(solution)/shard_map/all_to_all | solution.py:78
  101.8 2.6 %fusion.18 = (f32[256]{0:T(256)S(1)}, f32[256,1024]{1,0:T(8,128)S(1)}) fusion(s32[1024]{0:T(1024)S(1)} %add_select_fusion.1, s32[256]{0:T(256)S(1)} %eq.52, pred[1024]{0:T(1024)(128)(4,1)S(1)} %fusion.30, f32[1024]{0:T(1024)S(1)} %bitcast.61, bf16[256,1024]{1,0:T(8,128)(2,1)S(1)} %reshape.226, bf16[1024,1024]{1,0:T(8,128)(2,1)} %bitcast.55), kind=kOutput, calls=%fused_computation.37 | convolution fusion | flops 538705664 | bytes 3681280 | tf_op jit(solution)/shard_map/while/body/eval_jaxpr/dot_general | solution.py:16
  105.8 2.1 convolution_convert_fusion.1
  108.5 8.5 %psum.14 = f32[8,128]{1,0:T(8,128)S(1)} all-reduce(f32[8,128]{1,0:T(8,128)S(1)} %bitcast.60), channel_id=1, replica_groups=mesh['rows'=128,'rep'=4] {'rep'}, use_global_device_ids=true, to_apply=%region_5.6 | all-reduce | flops 1024 | bytes 8192 | tf_op jit(solution)/shard_map/psum | solution.py:94
  117.1 21.9 %reduce-scatter.3.cloned.1.call-done = bf16[8,32,1024]{2,1,0:T(8,128)(2,1)} async-done(((bf16[8,128,1024]{2,1,0:T(8,128)(2,1)}), bf16[8,32,1024]{2,1,0:T(8,128)(2,1)}) %reduce-scatter.3.cloned.1.call-update) | async-done | bytes 524304 | tf_op jit(solution)/shard_map/reduce_scatter | solution.py:91
  139.0 2.2 divide_convert_fusion
  141.3 38.9 %all-gather.2.cloned.1.call-done = bf16[8,128,1024]{2,1,0:T(8,128)(2,1)} async-done(((bf16[8,32,1024]{2,1,0:T(8,128)(2,1)}), bf16[8,128,1024]{2,1,0:T(8,128)(2,1)}) %all-gather.2.cloned.1.call-update) | async-done | bytes 2097168 | tf_op jit(solution)/shard_map/all_gather | solution.py:101
  180.1 2.2 multiply_reduce_fusion
  184.6 2.0 convolution_convert_fusion
  188.0 16.6 %all-to-all-start.3 = ((f32[128,1,2]{2,1,0:T(1,128)}), f32[128,1,2]{2,1,0:T(1,128)S(1)}, u32[]{:S(2)}, u32[]{:S(2)}) async-start(f32[128,1,2]{2,1,0:T(1,128)} %bitcast.16), calls=%async_computation.5 | async-start | bytes 131072 | tf_op jit(solution)/shard_map/all_to_all | solution.py:102
  205.2 7.5 %psum.15 = f32[8,128]{1,0:T(8,128)S(1)} all-reduce(f32[8,128]{1,0:T(8,128)S(1)} %bitcast.59), channel_id=1, replica_groups=mesh['rows'=128,'rep'=4] {'rep'}, use_global_device_ids=true, to_apply=%region_11.12 | all-reduce | flops 1024 | bytes 8192 | tf_op jit(solution)/shard_map/psum | solution.py:94
  212.7 6.7 %all-to-all-done.3 = f32[128,1,2]{2,1,0:T(1,128)S(1)} async-done(((f32[128,1,2]{2,1,0:T(1,128)}), f32[128,1,2]{2,1,0:T(1,128)S(1)}, u32[]{:S(2)}, u32[]{:S(2)}) %all-to-all-start.3) | async-done | bytes 1056 | tf_op jit(solution)/shard_map/all_to_all | solution.py:102
  220.9 2.8 %scatter_custom_fusion = f32[128]{0:T(128)} fusion(s32[256]{0:T(256)S(1)} %bitcast.65, f32[256]{0:T(256)S(1)} %broadcast_select_fusion, f32[]{:T(128)} %constant.93.clone.1), kind=kCustom, calls=%fused_computation.67 | custom fusion | flops 256 | bytes 516 | tf_op jit(solution)/shard_map/scatter-add | solution.py:107
  224.5 2.4 %add_divide_fusion = f32[8,32,1024]{2,1,0:T(8,128)} fusion(bf16[8,32,1024]{2,1,0:T(8,128)(2,1)} %reduce-scatter.5.cloned.1.call-done, f32[8,32]{1,0:T(8,128)S(1)} %dynamic-slice_add_fusion, bf16[8,128,1024]{2,1,0:T(8,128)(2,1)} %all-gather.2.cloned.1.call-done, s32[]{:T(128)S(6)} %select_n.113), kind=kLoop, calls=%fused_computation.26 | loop fusion | flops 1048576 | bytes 2098180 | tf_op jit(solution)/shard_map/div | solution.py:99
  (57 shorter events, 13.5 us)
Async XLA Ops:
  7.2 42.5 %copy-start = (bf16[128,1024]{1,0:T(8,128)(2,1)S(1)}, bf16[128,1024]{1,0:T(8,128)(2,1)}, u32[]{:S(2)}) copy-start(bf16[128,1024]{1,0:T(8,128)(2,1)} %param.6) | copy-start | bytes 786436
  7.2 23.0 %copy-start.1 = (s32[128]{0:T(128)S(1)}, s32[128]{0:T(128)}, u32[]{:S(2)}) copy-start(s32[128]{0:T(128)} %param.7) | copy-start | bytes 1540
  8.6 35.4 %all-to-all-start.2 = ((s32[128,1,1]{2,1,0:T(1,128)}), s32[128,1,1]{2,1,0:T(1,128)S(1)}, u32[]{:S(2)}, u32[]{:S(2)}) async-start(s32[128,1,1]{2,1,0:T(1,128)} %copy.23), calls=%async_computation.2 | async-start | bytes 131072 | tf_op jit(solution)/shard_map/all_to_all | solution.py:80
  44.0 20.6 %all-to-all-start = ((s32[128,1,2]{2,1,0:T(1,128)}), s32[128,1,2]{2,1,0:T(1,128)S(1)}, u32[]{:S(2)}, u32[]{:S(2)}) async-start(s32[128,1,2]{2,1,0:T(1,128)} %bitcast.1), calls=%async_computation | async-start | bytes 131072 | tf_op jit(solution)/shard_map/all_to_all | solution.py:79
  50.9 19.7 %copy-start.5 = (s32[8]{0:T(128)S(1)}, s32[8]{0:T(128)}, u32[]{:S(2)}) copy-start(s32[8]{0:T(128)} %param.10) | copy-start | bytes 100
  64.7 37.0 %all-to-all-start.1 = ((bf16[128,2,1024]{2,1,0:T(2,128)(2,1)}), bf16[128,2,1024]{2,1,0:T(2,128)(2,1)S(1)}, u32[]{:S(2)}, u32[]{:S(2)}) async-start(bf16[128,2,1024]{2,1,0:T(2,128)(2,1)} %reshape.241), calls=%async_computation.1 | async-start | bytes 1048576 | tf_op jit(solution)/shard_map/all_to_all | solution.py:78
  70.3 68.7 %reduce-scatter.3.cloned.1.call-start = ((), (), s32[]{:S(2)}) async-start(), calls=%async_computation.6 | async-start | bytes 2621440 | tf_op jit(solution)/shard_map/reduce_scatter | solution.py:91
  107.9 72.2 %all-gather.2.cloned.1.call-start = ((), (), s32[]{:S(2)}) async-start(), calls=%async_computation.7 | async-start | bytes 2621440 | tf_op jit(solution)/shard_map/all_gather | solution.py:101
  141.2 83.3 %reduce-scatter.5.cloned.1.call-start = ((), (), s32[]{:S(2)}) async-start(), calls=%async_computation.8 | async-start | bytes 2621440 | tf_op jit(solution)/shard_map/reduce_scatter | solution.py:91
  180.1 2.2 copy-start.2
  184.6 2.1 copy-start.3
  184.6 2.2 copy-start.4
  188.0 31.5 %all-to-all-start.3 = ((f32[128,1,2]{2,1,0:T(1,128)}), f32[128,1,2]{2,1,0:T(1,128)S(1)}, u32[]{:S(2)}, u32[]{:S(2)}) async-start(f32[128,1,2]{2,1,0:T(1,128)} %bitcast.16), calls=%async_computation.5 | async-start | bytes 131072 | tf_op jit(solution)/shard_map/all_to_all | solution.py:102
Sparse Core Ops, SparseCore 0:
  108.0 30.9 reduce-scatter.2
  141.9 38.2 all-gather.1
  186.8 37.6 reduce-scatter.4
where the time goes:
time: 234 us; the launch traced here: 233 us
  waiting for transfers between devices  117 us (50%)
  starting transfers between devices  48.8 us (21%)
  other arithmetic  20.6 us (9%)
  blocking collectives  15.9 us (7%)
  between operations  14 us (6%)
  local copies, waits for them, and re-layouts  9.3 us (4%)
  matrix products  7.63 us (3%)
    all_gather x1, waiting for transfers between devices, on_device(): lax.all_gather(updated.astype(jnp.bfloat16), 'rep', axis=1, tiled=True)  38.9 us
    all_to_all x1, waiting for transfers between devices, deliver(): lax.all_to_all(outgoing, 'rows', split_axis=0, concat_axis=0, tiled=True)  24.8 us
    reduce_scatter x2, waiting for transfers between devices, on_device(): lax.psum_scatter(sum_acc.astype(jnp.bfloat16), 'rep', scatter_dimension=1...  22.7 us
    all_to_all x1, starting transfers between devices, deliver(): lax.all_to_all(counting, 'rows', split_axis=0, concat_axis=0, tiled=True)  20.6 us
    all_to_all x1, starting transfers between devices, on_device(): lax.all_to_all(energy_slots, 'rows', split_axis=0, concat_axis=0, tiled=T...  16.6 us
    psum x2, blocking collectives, on_device(): full_weights = lax.psum(weight_acc, 'rep')  15.9 us
    all_to_all x1, waiting for transfers between devices, deliver(): lax.all_to_all(sub_parent, 'rows', split_axis=0, concat_axis=0, tiled=True)  12.8 us
    all_to_all x1, waiting for transfers between devices, deliver(): lax.all_to_all(counting, 'rows', split_axis=0, concat_axis=0, tiled=True)  11.2 us
  transfers between devices with their start and end apart: 7, of which 7 were waited for; matrix products, arithmetic and copies ran while one was open for 8% of the time, Pallas kernels for 0%

commit v1 on v0

v1 whole, which is shorter than its diff:
```python
import functools

import jax
import jax.numpy as jnp
from jax import lax
from jax.experimental import pallas as pl
from jax.experimental.pallas import tpu as pltpu
from jax.sharding import PartitionSpec as P

MESH = pl.DeviceIdType.MESH
F32 = jnp.float32
BF16 = jnp.bfloat16

NZ, NG, NQ = 16, 8, 4
NR = NZ * NG
HALF = NZ // 2
PAR, SHARE, D = 8, 32, 1024
COLS = PAR * SHARE
FLOOR = -1e30
TEMP = 1.0 / 32.0


def dz_of(s):
    odd = s % 2
    d = HALF - (s + 1) // 2
    return odd * d + (1 - odd) * (NZ - d)


def sdz(s):
    odd = lax.rem(s, 2)
    d = HALF - lax.div(s + 1, 2)
    return odd * d + (1 - odd) * (NZ - d)


def mult(x, m):
    return pl.multiple_of(x, m)


def iota(shape, dim):
    return lax.broadcasted_iota(jnp.int32, shape, dim)


def kernel(
    emb, listing, counting, parent, ccount, cent,
    out, energy,
    stage, tiles, xg, rows_f, xs, panel, norms, lg, resp, wsum,
    meta_o, zb, sb, yb, mx, xm,
    sx, rx, est, eb, fs, fb, fo,
    pan_sem, zss, zrs, xss, xrl, xrr, xrf, mss, mzr, myr, mxr, sss, srs, ess, ezr, eyr,
):
    r = lax.axis_index("rows")
    q = lax.axis_index("rep")
    z = lax.div(r, NG)
    g = lax.rem(r, NG)
    right = lax.rem(q + 1, NQ)
    left = lax.rem(q + 3, NQ)
    opp = lax.rem(q + 2, NQ)

    def remote(src, dst, ss, rs, dev):
        return pltpu.make_async_remote_copy(
            src_ref=src, dst_ref=dst, send_sem=ss, recv_sem=rs, device_id=dev, device_id_type=MESH
        )

    barrier = pltpu.get_barrier_semaphore()

    @pl.loop(1, NR)
    def _(i):
        pl.semaphore_signal(
            barrier, inc=1, device_id=(lax.rem(r + i, NR), q), device_id_type=MESH
        )

    for peer in (right, left, opp):
        pl.semaphore_signal(barrier, inc=1, device_id=(r, peer), device_id_type=MESH)

    load = pltpu.make_async_copy(cent.at[:, pl.ds(mult(q * SHARE, SHARE), SHARE), :], panel, pan_sem)
    load.start()

    lane = iota((NR, NR), 1)
    row_i = iota((NR, NR), 0)
    count_col = jnp.sum(jnp.where(lane == row_i, counting[...].astype(F32), 0.0), axis=1, keepdims=True)
    par_row = lax.rem(parent[...], PAR).astype(F32)
    hots = []
    meta = jnp.zeros((NR, NR), F32)
    for j in range(2):
        hot = (lane == listing[:, j : j + 1]) & (count_col > j)
        hots.append(hot)
        code = jnp.sum(jnp.where(hot, par_row + 1.0, 0.0), axis=1, keepdims=True)
        meta = meta + jnp.where(lax.rem(lane, 16) == g * 2 + j, code, 0.0)
        picked = jnp.dot(hot.astype(BF16), emb[...], preferred_element_type=F32)
        for k in range(8):
            stage[pl.ds(j * 8 + k, NR, stride=16), :] = picked[:, 128 * k : 128 * (k + 1)]
    tiles[...] = stage[...].astype(BF16)
    meta_o[...] = meta

    load.wait()
    for p in range(PAR):
        wide = panel[p].astype(F32)
        norms[p * SHARE : (p + 1) * SHARE, :] = jnp.sum(wide * wide, axis=1, keepdims=True)

    pl.semaphore_wait(barrier, NR - 1 + NQ - 1)

    def send_rows(s, i):
        zt = lax.rem(z + sdz(s), NZ)
        o = zt * NG + lax.rem(g + i, NG)
        remote(
            tiles.at[pl.ds(mult(o * 16, 16), 16)],
            xg.at[pl.ds(mult((s * NQ + q) * 128 + g * 16, 16), 16)],
            zss, zrs.at[s], (o, q),
        ).start()

    def send_steps(first, last):
        @pl.loop(first, last)
        def _(s):
            @pl.loop(0, NG)
            def _(i):
                send_rows(s, i)

    send_steps(0, 2)

    @pl.loop(0, NZ - 1)
    def _(s):
        zt = lax.rem(z + sdz(s), NZ)
        remote(
            meta_o.at[pl.ds(mult(zt * NG, 8), 8)], zb.at[pl.ds(mult(s * 8, 8), 8)],
            mss, mzr, (zt * NG + g, q),
        ).start()

    send_steps(2, NZ - 1)

    @pl.loop(1, NG)
    def _(i):
        send_rows(NZ - 1, i)

    xg[pl.ds(mult(((NZ - 1) * NQ + q) * 128 + g * 16, 16), 16), :] = tiles[pl.ds(mult(r * 16, 16), 16), :]
    zb[(NZ - 1) * 8 :, :] = meta_o[pl.ds(mult(z * 8, 8), 8), :]

    def chunk(t, qq):
        return xg.at[pl.ds(mult((t * NQ + qq) * 128, 128), 128)]

    def step(s):
        @pl.when(s < NZ)
        def _():
            @pl.when(s < NZ - 1)
            def _():
                remote(chunk(s, q), chunk(s, q), zss, zrs.at[s], (r, right)).wait_recv()

            @pl.when(s == NZ - 1)
            def _():
                part = xg.at[pl.ds(0, 112)]
                remote(part, part, zss, zrs.at[s], (r, right)).wait_recv()

            remote(chunk(s, q), chunk(s, q), xss, xrl.at[s], (r, right)).start()
            remote(chunk(s, q), chunk(s, q), xss, xrr.at[s], (r, left)).start()

        @pl.when((s >= 1) & (s <= NZ))
        def _():
            t = s - 1
            remote(chunk(t, q), chunk(t, left), xss, xrl.at[t], (r, right)).wait_recv()
            remote(chunk(t, q), chunk(t, right), xss, xrr.at[t], (r, left)).wait_recv()

            @pl.when(lax.rem(t, 2) == 0)
            def _():
                remote(chunk(t, left), chunk(t, left), xss, xrf.at[t], (r, right)).start()

            @pl.when(lax.rem(t, 2) == 1)
            def _():
                remote(chunk(t, right), chunk(t, right), xss, xrf.at[t], (r, left)).start()

        @pl.when(s >= 2)
        def _():
            t = s - 2
            remote(chunk(t, q), chunk(t, opp), xss, xrf.at[t], (r, right)).wait_recv()
            half = lax.div(t, HALF)
            place = half * 512 + lax.rem(t, HALF) * 16
            for qq in range(NQ):
                rows_f[qq * 128 : (qq + 1) * 128, :] = xg[
                    pl.ds(mult((t * NQ + qq) * 128, 128), 128), :
                ].astype(F32)
                for k in range(8):
                    xs[pl.ds(mult(place + qq * 128, 16), 16), 128 * k : 128 * (k + 1)] = rows_f[
                        pl.ds(qq * 128 + k, 16, stride=8), :
                    ].astype(BF16)

    pl.loop(0, 4)(step)

    mate = meta_o.at[pl.ds(0, 120)]
    remote(mate, zb.at[pl.ds(0, 120)], mss, mzr, (r, right)).wait_recv()
    for gg in range(NG):
        sb[gg * 16 : (gg + 1) * 16, :] = zb[pl.ds(gg, 16, stride=8), :]

    @pl.loop(1, NG)
    def _(i):
        gt = lax.rem(g + i, NG)
        remote(
            sb.at[pl.ds(mult(gt * 16, 16), 16)], yb.at[pl.ds(mult(g * 16, 16), 16)],
            mss, myr, (z * NG + gt, q),
        ).start()

    yb[pl.ds(mult(g * 16, 16), 16), :] = sb[pl.ds(mult(g * 16, 16), 16), :]

    pl.loop(4, 6)(step)

    mate = sb.at[pl.ds(0, 112)]
    remote(mate, yb.at[pl.ds(0, 112)], mss, myr, (r, right)).wait_recv()
    slot = yb[0:16, :]
    for gg in range(1, NG):
        slot = slot + yb[gg * 16 : (gg + 1) * 16, :]
    sl = iota((16, 128), 0)
    ln = lax.div(iota((16, 128), 1), 16)
    for h in range(2):
        mx[h : h + 1, :] = jnp.sum(jnp.where(sl == h * HALF + ln, slot, 0.0), axis=0, keepdims=True)
    mx[2:8, :] = jnp.zeros((6, 128), F32)
    for k, peer in enumerate((right, left, opp)):
        remote(mx, xm.at[pl.ds(mult(q * 8, 8), 8)], mss, mxr, (r, peer)).start()
    xm[pl.ds(mult(q * 8, 8), 8), :] = mx[...]

    pl.loop(6, 8)(step)

    mate = xm.at[pl.ds(0, 24)]
    remote(mate, mate, mss, mxr, (r, right)).wait_recv()

    kid = iota((SHARE, 1), 0) + q * SHARE

    def codes(h):
        return jnp.concatenate([xm[qq * 8 + h : qq * 8 + h + 1, :] for qq in range(NQ)], axis=1)

    def local_softmax(it, h):
        lg[...] = lax.dot_general(
            panel[...].reshape(COLS, D), xs[h * 512 : (h + 1) * 512, :],
            (((1,), (1,)), ((), ())), preferred_element_type=F32,
        )
        code = codes(h)
        top = jnp.full((1, 512), FLOOR, F32)
        for p in range(PAR):
            rows = slice(p * SHARE, (p + 1) * SHARE)
            allowed = (code == p + 1.0) & (kid < ccount[p])
            logits = jnp.where(allowed, (2.0 * lg[rows, :] - norms[rows, :]) * TEMP, FLOOR)
            lg[rows, :] = logits
            top = jnp.maximum(top, jnp.max(logits, axis=0, keepdims=True))
        total = jnp.zeros((1, 512), F32)
        for p in range(PAR):
            rows = slice(p * SHARE, (p + 1) * SHARE)
            logits = lg[rows, :]
            terms = jnp.where(logits > 0.5 * FLOOR, jnp.exp(logits - top), 0.0)
            resp[rows, h * 512 : (h + 1) * 512] = terms
            total = total + jnp.sum(terms, axis=0, keepdims=True)
        base = (it * 2 + h) * 8
        for qq in range(NQ):
            sx[base + qq : base + qq + 1, :] = top[:, qq * 128 : (qq + 1) * 128]
            sx[base + 4 + qq : base + 5 + qq, :] = total[:, qq * 128 : (qq + 1) * 128]
        for k, peer in enumerate((right, left, opp)):
            remote(
                sx.at[pl.ds(base, 8)], rx.at[pl.ds((it * 2 + h) * 24 + k * 8, 8)],
                sss, srs.at[(it * 2 + h) * 3 + k], (r, peer),
            ).start()

    def whole_softmax(it, h):
        base = (it * 2 + h) * 8
        mine = sx[base : base + 8, :]
        top = mine[0:4]
        others = []
        for k in range(3):
            at = (it * 2 + h) * 24 + k * 8
            remote(
                sx.at[pl.ds(base, 8)], rx.at[pl.ds(at, 8)], sss, srs.at[(it * 2 + h) * 3 + k], (r, right)
            ).wait_recv()
            others.append(rx[at : at + 8, :])
        for other in others:
            top = jnp.maximum(top, other[0:4])
        own = jnp.exp(mine[0:4] - top)
        total = mine[4:8] * own
        for other in others:
            total = total + other[4:8] * jnp.exp(other[0:4] - top)
        live = jnp.concatenate([xm[qq * 8 + h : qq * 8 + h + 1, :] for qq in range(NQ)], axis=0) > 0.5
        scale = jnp.where(live, own / total, 0.0)
        return scale, top + jnp.log(total)

    def weigh(h, scale):
        weights = jnp.zeros((COLS, 1), F32)
        for qq in range(NQ):
            cols = slice(h * 512 + qq * 128, h * 512 + (qq + 1) * 128)
            full = resp[:, cols] * scale[qq : qq + 1, :]
            resp[:, cols] = full
            weights = weights + jnp.sum(full, axis=1, keepdims=True)
        return weights

    pl.loop(8, 10)(step)
    local_softmax(0, 0)
    pl.loop(10, NZ + 2)(step)
    local_softmax(0, 1)

    for it in range(2):
        if it == 1:
            local_softmax(1, 0)
            local_softmax(1, 1)
        weights = jnp.zeros((COLS, 1), F32)
        for h in range(2):
            scale, full_energy = whole_softmax(it, h)
            if it == 1:
                own_row = jnp.sum(
                    jnp.where(iota((NQ, 128), 0) == q, full_energy, 0.0), axis=0, keepdims=True
                )
                est[h * 8 : (h + 1) * 8, :] = jnp.broadcast_to(own_row, (8, 128))

                @pl.loop(h * HALF, (h + 1) * HALF - h)
                def _(s):
                    zt = lax.rem(z + NZ - sdz(s), NZ)
                    remote(
                        est.at[pl.ds(h * 8, 8)], eb.at[pl.ds(mult(z * 8, 8), 8)],
                        ess, ezr, (zt * NG + g, q),
                    ).start()

            weights = weights + weigh(h, scale)
        inverse = 1.0 / (weights + 1.0)
        half_resp = resp[...].astype(BF16)
        square = jnp.zeros((COLS, 1), F32)
        for b in range(4):
            cols = slice(b * 256, (b + 1) * 256)
            sums = jnp.dot(half_resp, xs[:, cols], preferred_element_type=F32)
            old = panel[:, :, cols].reshape(COLS, 256).astype(F32)
            new = (sums + old) * inverse
            if it == 0:
                low = new.astype(BF16)
                panel[:, :, cols] = low.reshape(PAR, SHARE, 256)
                wide = low.astype(F32)
                square = square + jnp.sum(wide * wide, axis=1, keepdims=True)
            else:
                out[:, :, cols] = new.reshape(PAR, SHARE, 256)
        if it == 0:
            norms[...] = square

    mate = eb.at[pl.ds(0, 120)]
    remote(mate, mate, ess, ezr, (r, right)).wait_recv()
    eb[pl.ds(mult(z * 8, 8), 8), :] = est[8:16, :]
    fs[...] = eb[pl.ds(0, 16, stride=8), :]

    @pl.loop(1, NG)
    def _(i):
        gt = lax.rem(g + i, NG)
        remote(fs, fb.at[pl.ds(mult(g * 16, 16), 16)], ess, eyr, (z * NG + gt, q)).start()

    mate = fb.at[pl.ds(0, 112)]
    remote(mate, mate, ess, eyr, (r, right)).wait_recv()
    fb[pl.ds(mult(g * 16, 16), 16), :] = fs[...]
    for gg in range(NG):
        fo[pl.ds(gg, 16, stride=8), :] = fb[gg * 16 : (gg + 1) * 16, :]
    dz = lax.rem(lax.div(row_i, NG) + NZ - z, NZ)
    s_of = jnp.where(dz < HALF, NZ - 1 - 2 * dz, 2 * dz - NZ)
    at = lax.rem(s_of, HALF) * 16 + g * 2
    home = jnp.zeros((1, NR), F32)
    for j in range(2):
        hot = (lane == listing[:, j : j + 1]) & (count_col > j)
        value = jnp.sum(jnp.where(lane == at + j, fo[...], 0.0), axis=1, keepdims=True)
        home = home + jnp.sum(jnp.where(hot, value, 0.0), axis=0, keepdims=True)
    energy[...] = home

    def drain(ref, sem):
        remote(ref, ref, sem, pan_sem, (r, right)).wait_send()

    drain(tiles.at[pl.ds(0, 127 * 16)], zss)
    drain(xg.at[pl.ds(0, 48 * 128)], xss)
    drain(stage.at[pl.ds(0, 256)], mss)
    drain(rx, sss)
    drain(stage.at[pl.ds(0, 232)], ess)


def on_device(embeddings, parent_id, send_list, send_count, child_count, centroids):
    dma = pltpu.SemaphoreType.DMA
    vmem = pl.BlockSpec(memory_space=pltpu.VMEM)
    updated, row_energy = pl.pallas_call(
        kernel,
        name="refine",
        out_shape=(
            jax.ShapeDtypeStruct((PAR, SHARE, D), F32),
            jax.ShapeDtypeStruct((1, NR), F32),
        ),
        in_specs=[
            vmem, vmem, vmem, vmem,
            pl.BlockSpec(memory_space=pltpu.SMEM),
            pl.BlockSpec(memory_space=pl.ANY),
        ],
        out_specs=(vmem, vmem),
        scratch_shapes=[
            pltpu.VMEM((2048, 128), F32),
            pltpu.VMEM((2048, 128), BF16),
            pltpu.VMEM((64 * 128, 128), BF16),
            pltpu.VMEM((512, 128), F32),
            pltpu.VMEM((1024, D), BF16),
            pltpu.VMEM((PAR, SHARE, D), BF16),
            pltpu.VMEM((COLS, 1), F32),
            pltpu.VMEM((COLS, 512), F32),
            pltpu.VMEM((COLS, 1024), F32),
            pltpu.VMEM((8, 128), F32),
            pltpu.VMEM((128, 128), F32),
            pltpu.VMEM((128, 128), F32),
            pltpu.VMEM((128, 128), F32),
            pltpu.VMEM((128, 128), F32),
            pltpu.VMEM((8, 128), F32),
            pltpu.VMEM((32, 128), F32),
            pltpu.VMEM((32, 128), F32),
            pltpu.VMEM((96, 128), F32),
            pltpu.VMEM((16, 128), F32),
            pltpu.VMEM((128, 128), F32),
            pltpu.VMEM((16, 128), F32),
            pltpu.VMEM((128, 128), F32),
            pltpu.VMEM((128, 128), F32),
            dma, dma, dma((NZ,)), dma, dma((NZ,)), dma((NZ,)), dma((NZ,)),
            dma, dma, dma, dma,
            dma, dma((12,)),
            dma, dma, dma,
        ],
        compiler_params=pltpu.CompilerParams(
            collective_id=0, has_side_effects=True, vmem_limit_bytes=40 * 1024 * 1024
        ),
    )(
        embeddings,
        send_list[0],
        send_count,
        parent_id[None, :],
        child_count,
        centroids,
    )
    return (updated, row_energy[0])


def solution(mesh):
    in_specs = (
        P(("rows", "rep"), None),
        P(("rows", "rep")),
        P(("rows", "rep"), None, None),
        P(("rows", "rep"), None),
        P("rows"),
        P("rows", None, None),
    )
    out_specs = (P("rows", "rep", None), P(("rows", "rep")))
    return jax.shard_map(
        on_device, mesh=mesh, in_specs=in_specs, out_specs=out_specs, check_vma=False
    )
```

time: 234 us -> 105 us (0.45)
  waiting for transfers between devices: 117 us -> 0 us
  Pallas kernels: 0 us -> 97 us
  starting transfers between devices: 48.8 us -> 0 us
  other arithmetic: 20.6 us -> 0 us
  blocking collectives: 15.9 us -> 0 us
  between operations: 14 us -> 0.65 us
  matrix products: 7.63 us -> 0 us
  local copies, waits for them, and re-layouts: 9.3 us -> 6.77 us
    pallas_call x0 -> x1, Pallas kernels: none -> 97 us  [on_device(): pl.pallas_call(kernel, name='refine', out_shape=(jax.ShapeDtypeStruct((PA...]
    all_to_all x4 -> x0, waiting for transfers between devices: 55.5 us -> none  [the longest x1 24.8 us: deliver(): lax.all_to_all(outgoing, 'rows', split_axis=0, concat_axis=0, tiled=True)]
    all_to_all x4 -> x0, starting transfers between devices: 48.5 us -> none  [the longest x1 20.6 us: deliver(): lax.all_to_all(counting, 'rows', split_axis=0, concat_axis=0, tiled=True)]
    all_gather x1 -> x0, waiting for transfers between devices: 38.9 us -> none  [on_device(): lax.all_gather(updated.astype(jnp.bfloat16), 'rep', axis=1, tiled=True)]
    reduce_scatter x2 -> x0, waiting for transfers between devices: 22.7 us -> none  [on_device(): lax.psum_scatter(sum_acc.astype(jnp.bfloat16), 'rep', scatter_dimension=1...]
    psum x2 -> x0, blocking collectives: 15.9 us -> none  [on_device(): full_weights = lax.psum(weight_acc, 'rep')]
    dot_general x4 -> x0, matrix products: 7.63 us -> none  [the longest x2 4.08 us: block_terms(): jnp.dot(weights_half.T, row_block, preferred_element_type=jnp.float32)]
    unnamed x13, local copies, waits for them, and re-layouts: 0.15 us -> 6.77 us
  transfers between devices with their start and end apart: 7 -> 0, of which waited for: 7 -> 0; matrix products, arithmetic and copies ran while one was open for 8% -> 0% of each run, Pallas kernels for 0% -> 0%
where the time goes in v1:
time: 105 us; the launch traced here: 104 us
  Pallas kernels  97 us (92%)
  local copies, waits for them, and re-layouts  6.77 us (6%)
    pallas_call x1, Pallas kernels, on_device(): pl.pallas_call(kernel, name='refine', out_shape=(jax.ShapeDtypeStruct((PA...  97 us
    unnamed x13, local copies, waits for them, and re-layouts  6.77 us

profile of v1, /device:TPU:1, one launch (start us, length us, event | category | flops | bytes accessed | tf_op | source)
XLA Modules:
  0.0 104.5 jit_solution(14185003055378644029)
XLA Ops:
  0.6 0.8 copy.8
  1.4 0.0 copy-start
  1.4 1.6 %copy-done = bf16[8,128,1024]{2,1,0:T(8,128)(2,1)S(1)} copy-done((bf16[8,128,1024]{2,1,0:T(8,128)(2,1)S(1)}, bf16[8,128,1024]{2,1,0:T(8,128)(2,1)}, u32[]{:S(2)}) %copy-start) | copy-done | bytes 2097176
  3.0 0.0 copy-start.1
  3.0 0.9 copy-done.1
  4.0 0.0 copy-start.2
  4.0 0.7 copy-done.2
  4.6 0.0 copy-start.3
  4.6 0.7 copy-done.3
  5.3 0.0 copy-start.4
  5.3 0.7 copy-done.4
  5.9 97.0 %refine.1 = (f32[8,32,1024]{2,1,0:T(8,128)S(1)}, f32[1,128]{1,0:T(1,128)S(1)}) custom-call(bf16[128,1024]{1,0:T(8,128)(2,1)S(1)} %copy-done.1, s32[128,2]{1,0:T(8,128)S(1)} %bitcast.3, s32[1,128]{1,0:T(1,128)S(1)} %copy-done.2, s32[1,128]{1,0:T(1,128)S(1)} %bitcast.4, s32[8]{0:T(128)S(1)} %copy-done.4, bf16[8,128,1024]{2,1,0:T(8,128)(2,1)S(1)} %copy-done), custom_call_target="tpu_custom_call" | custom-call | tf_op jit(solution)/shard_map/refine/pallas_call | solution.py:370
  103.0 1.0 copy.11
  103.9 0.5 copy.12
Async XLA Ops:
  1.4 1.6 %copy-start = (bf16[8,128,1024]{2,1,0:T(8,128)(2,1)S(1)}, bf16[8,128,1024]{2,1,0:T(8,128)(2,1)}, u32[]{:S(2)}) copy-start(bf16[8,128,1024]{2,1,0:T(8,128)(2,1)} %cent.1) | copy-start | bytes 6291460
  3.0 0.9 copy-start.1
  4.0 0.7 copy-start.2
  4.6 0.7 copy-start.3
  5.3 0.7 copy-start.4

commit v2 on v1

--- a/solution.py
+++ b/solution.py
@@ -17,19 +17,13 @@
 PAR, SHARE, D = 8, 32, 1024
 COLS = PAR * SHARE
 FLOOR = -1e30
+LEAD, LAG1, LAG2 = 4, 2, 4
 TEMP = 1.0 / 32.0
-
-
-def dz_of(s):
-    odd = s % 2
-    d = HALF - (s + 1) // 2
-    return odd * d + (1 - odd) * (NZ - d)
 
 
 def sdz(s):
     odd = lax.rem(s, 2)
-    d = HALF - lax.div(s + 1, 2)
-    return odd * d + (1 - odd) * (NZ - d)
+    return odd * lax.div(s + 1, 2) + (1 - odd) * (NZ - lax.div(s, 2))
 
 
 def mult(x, m):
@@ -41,12 +35,13 @@
 
 
 def kernel(
-    emb, listing, counting, parent, ccount, cent,
+    emb_hbm, listing_hbm, counting_hbm, parent_hbm, ccount_hbm, cent,
     out, energy,
-    stage, tiles, xg, rows_f, xs, panel, norms, lg, resp, wsum,
+    emb, listing, counting, parent, ccount,
+    stage, tiles, xg, rows_f, xs, panel, norms, lg, resp,
     meta_o, zb, sb, yb, mx, xm,
     sx, rx, est, eb, fs, fb, fo,
-    pan_sem, zss, zrs, xss, xrl, xrr, xrf, mss, mzr, myr, mxr, sss, srs, ess, ezr, eyr,
+    in_sem, zss, zrs, xss, xrl, xrr, xrf, mss, mzr, myr, mxr, sss, srs, ess, ezr, eyr,
 ):
     r = lax.axis_index("rows")
     q = lax.axis_index("rep")
@@ -61,6 +56,20 @@
             src_ref=src, dst_ref=dst, send_sem=ss, recv_sem=rs, device_id=dev, device_id_type=MESH
         )
 
+    loads = [
+        pltpu.make_async_copy(src, dst, in_sem.at[k])
+        for k, (src, dst) in enumerate((
+            (emb_hbm, emb),
+            (listing_hbm, listing),
+            (counting_hbm, counting),
+            (parent_hbm, parent),
+            (ccount_hbm, ccount),
+            (cent.at[:, pl.ds(mult(q * SHARE, SHARE), SHARE), :], panel),
+        ))
+    ]
+    for load in loads:
+        load.start()
+
     barrier = pltpu.get_barrier_semaphore()
 
     @pl.loop(1, NR)
@@ -72,18 +81,20 @@
     for peer in (right, left, opp):
         pl.semaphore_signal(barrier, inc=1, device_id=(r, peer), device_id_type=MESH)
 
-    load = pltpu.make_async_copy(cent.at[:, pl.ds(mult(q * SHARE, SHARE), SHARE), :], panel, pan_sem)
-    load.start()
+    for load in loads:
+        load.wait()
 
     lane = iota((NR, NR), 1)
     row_i = iota((NR, NR), 0)
     count_col = jnp.sum(jnp.where(lane == row_i, counting[...].astype(F32), 0.0), axis=1, keepdims=True)
     par_row = lax.rem(parent[...], PAR).astype(F32)
-    hots = []
+    listed = []
+    for j in range(2):
+        wide = jnp.where(lane == row_i, listing[j : j + 1, :].astype(F32), 0.0)
+        listed.append(jnp.sum(wide, axis=1, keepdims=True).astype(jnp.int32))
     meta = jnp.zeros((NR, NR), F32)
     for j in range(2):
-        hot = (lane == listing[:, j : j + 1]) & (count_col > j)
-        hots.append(hot)
+        hot = (lane == listed[j]) & (count_col > j)
         code = jnp.sum(jnp.where(hot, par_row + 1.0, 0.0), axis=1, keepdims=True)
         meta = meta + jnp.where(lax.rem(lane, 16) == g * 2 + j, code, 0.0)
         picked = jnp.dot(hot.astype(BF16), emb[...], preferred_element_type=F32)
@@ -92,7 +103,6 @@
     tiles[...] = stage[...].astype(BF16)
     meta_o[...] = meta
 
-    load.wait()
     for p in range(PAR):
         wide = panel[p].astype(F32)
         norms[p * SHARE : (p + 1) * SHARE, :] = jnp.sum(wide * wide, axis=1, keepdims=True)
@@ -108,31 +118,21 @@
             zss, zrs.at[s], (o, q),
         ).start()
 
-    def send_steps(first, last):
-        @pl.loop(first, last)
-        def _(s):
-            @pl.loop(0, NG)
-            def _(i):
-                send_rows(s, i)
-
-    send_steps(0, 2)
-
-    @pl.loop(0, NZ - 1)
-    def _(s):
+    @pl.loop(1, NG)
+    def _(i):
+        send_rows(0, i)
+
+    @pl.loop(1, NZ)
+    def _(k):
+        s = NZ - k
         zt = lax.rem(z + sdz(s), NZ)
         remote(
             meta_o.at[pl.ds(mult(zt * NG, 8), 8)], zb.at[pl.ds(mult(s * 8, 8), 8)],
             mss, mzr, (zt * NG + g, q),
         ).start()
 
-    send_steps(2, NZ - 1)
-
-    @pl.loop(1, NG)
-    def _(i):
-        send_rows(NZ - 1, i)
-
-    xg[pl.ds(mult(((NZ - 1) * NQ + q) * 128 + g * 16, 16), 16), :] = tiles[pl.ds(mult(r * 16, 16), 16), :]
-    zb[(NZ - 1) * 8 :, :] = meta_o[pl.ds(mult(z * 8, 8), 8), :]
+    xg[pl.ds(mult(q * 128 + g * 16, 16), 16), :] = tiles[pl.ds(mult(r * 16, 16), 16), :]
+    zb[0:8, :] = meta_o[pl.ds(mult(z * 8, 8), 8), :]
 
     def chunk(t, qq):
         return xg.at[pl.ds(mult((t * NQ + qq) * 128, 128), 128)]
@@ -140,11 +140,11 @@
     def step(s):
         @pl.when(s < NZ)
         def _():
-            @pl.when(s < NZ - 1)
+            @pl.when(s > 0)
             def _():
                 remote(chunk(s, q), chunk(s, q), zss, zrs.at[s], (r, right)).wait_recv()
 
-            @pl.when(s == NZ - 1)
+            @pl.when(s == 0)
             def _():
                 part = xg.at[pl.ds(0, 112)]
                 remote(part, part, zss, zrs.at[s], (r, right)).wait_recv()
@@ -152,9 +152,9 @@
             remote(chunk(s, q), chunk(s, q), xss, xrl.at[s], (r, right)).start()
             remote(chunk(s, q), chunk(s, q), xss, xrr.at[s], (r, left)).start()
 
-        @pl.when((s >= 1) & (s <= NZ))
+        @pl.when((s >= LAG1) & (s < NZ + LAG1))
         def _():
-            t = s - 1
+            t = s - LAG1
             remote(chunk(t, q), chunk(t, left), xss, xrl.at[t], (r, right)).wait_recv()
             remote(chunk(t, q), chunk(t, right), xss, xrr.at[t], (r, left)).wait_recv()
 
@@ -166,9 +166,9 @@
             def _():
                 remote(chunk(t, right), chunk(t, right), xss, xrf.at[t], (r, left)).start()
 
-        @pl.when(s >= 2)
+        @pl.when(s >= LAG2)
         def _():
-            t = s - 2
+            t = s - LAG2
             remote(chunk(t, q), chunk(t, opp), xss, xrf.at[t], (r, right)).wait_recv()
             half = lax.div(t, HALF)
             place = half * 512 + lax.rem(t, HALF) * 16
@@ -181,7 +181,15 @@
                         pl.ds(qq * 128 + k, 16, stride=8), :
                     ].astype(BF16)
 
-    pl.loop(0, 4)(step)
+    @pl.loop(1, NZ)
+    def _(s):
+        @pl.loop(0, NG)
+        def _(i):
+            send_rows(s, i)
+
+        @pl.when(s >= LEAD)
+        def _():
+            step(s - LEAD)
 
     mate = meta_o.at[pl.ds(0, 120)]
     remote(mate, zb.at[pl.ds(0, 120)], mss, mzr, (r, right)).wait_recv()
@@ -198,7 +206,7 @@
 
     yb[pl.ds(mult(g * 16, 16), 16), :] = sb[pl.ds(mult(g * 16, 16), 16), :]
 
-    pl.loop(4, 6)(step)
+    pl.loop(NZ - LEAD, NZ - LEAD + 1)(step)
 
     mate = sb.at[pl.ds(0, 112)]
     remote(mate, yb.at[pl.ds(0, 112)], mss, myr, (r, right)).wait_recv()
@@ -214,7 +222,7 @@
         remote(mx, xm.at[pl.ds(mult(q * 8, 8), 8)], mss, mxr, (r, peer)).start()
     xm[pl.ds(mult(q * 8, 8), 8), :] = mx[...]
 
-    pl.loop(6, 8)(step)
+    pl.loop(NZ - LEAD + 1, NZ - 1)(step)
 
     mate = xm.at[pl.ds(0, 24)]
     remote(mate, mate, mss, mxr, (r, right)).wait_recv()
@@ -284,9 +292,8 @@
             weights = weights + jnp.sum(full, axis=1, keepdims=True)
         return weights
 
-    pl.loop(8, 10)(step)
     local_softmax(0, 0)
-    pl.loop(10, NZ + 2)(step)
+    pl.loop(NZ - 1, NZ + LAG2)(step)
     local_softmax(0, 1)
 
     for it in range(2):
@@ -302,8 +309,9 @@
                 )
                 est[h * 8 : (h + 1) * 8, :] = jnp.broadcast_to(own_row, (8, 128))
 
-                @pl.loop(h * HALF, (h + 1) * HALF - h)
-                def _(s):
+                @pl.loop(1 - h, HALF)
+                def _(k):
+                    s = (h + 1) * HALF - 1 - k + (1 - h)
                     zt = lax.rem(z + NZ - sdz(s), NZ)
                     remote(
                         est.at[pl.ds(h * 8, 8)], eb.at[pl.ds(mult(z * 8, 8), 8)],
@@ -331,7 +339,7 @@
 
     mate = eb.at[pl.ds(0, 120)]
     remote(mate, mate, ess, ezr, (r, right)).wait_recv()
-    eb[pl.ds(mult(z * 8, 8), 8), :] = est[8:16, :]
+    eb[pl.ds(mult(z * 8, 8), 8), :] = est[0:8, :]
     fs[...] = eb[pl.ds(0, 16, stride=8), :]
 
     @pl.loop(1, NG)
@@ -345,17 +353,17 @@
     for gg in range(NG):
         fo[pl.ds(gg, 16, stride=8), :] = fb[gg * 16 : (gg + 1) * 16, :]
     dz = lax.rem(lax.div(row_i, NG) + NZ - z, NZ)
-    s_of = jnp.where(dz < HALF, NZ - 1 - 2 * dz, 2 * dz - NZ)
+    s_of = jnp.where((dz >= 1) & (dz <= HALF), 2 * dz - 1, lax.rem(2 * (NZ - dz), 2 * NZ))
     at = lax.rem(s_of, HALF) * 16 + g * 2
     home = jnp.zeros((1, NR), F32)
     for j in range(2):
-        hot = (lane == listing[:, j : j + 1]) & (count_col > j)
+        hot = (lane == listed[j]) & (count_col > j)
         value = jnp.sum(jnp.where(lane == at + j, fo[...], 0.0), axis=1, keepdims=True)
         home = home + jnp.sum(jnp.where(hot, value, 0.0), axis=0, keepdims=True)
     energy[...] = home
 
     def drain(ref, sem):
-        remote(ref, ref, sem, pan_sem, (r, right)).wait_send()
+        remote(ref, ref, sem, eyr, (r, right)).wait_send()
 
     drain(tiles.at[pl.ds(0, 127 * 16)], zss)
     drain(xg.at[pl.ds(0, 48 * 128)], xss)
@@ -374,13 +382,14 @@
             jax.ShapeDtypeStruct((PAR, SHARE, D), F32),
             jax.ShapeDtypeStruct((1, NR), F32),
         ),
-        in_specs=[
-            vmem, vmem, vmem, vmem,
-            pl.BlockSpec(memory_space=pltpu.SMEM),
-            pl.BlockSpec(memory_space=pl.ANY),
-        ],
+        in_specs=[pl.BlockSpec(memory_space=pltpu.HBM)] * 6,
         out_specs=(vmem, vmem),
         scratch_shapes=[
+            pltpu.VMEM((NR, D), BF16),
+            pltpu.VMEM((2, NR), jnp.int32),
+            pltpu.VMEM((1, NR), jnp.int32),
+            pltpu.VMEM((1, NR), jnp.int32),
+            pltpu.SMEM((PAR,), jnp.int32),
             pltpu.VMEM((2048, 128), F32),
             pltpu.VMEM((2048, 128), BF16),
             pltpu.VMEM((64 * 128, 128), BF16),
@@ -390,7 +399,6 @@
             pltpu.VMEM((COLS, 1), F32),
             pltpu.VMEM((COLS, 512), F32),
             pltpu.VMEM((COLS, 1024), F32),
-            pltpu.VMEM((8, 128), F32),
             pltpu.VMEM((128, 128), F32),
             pltpu.VMEM((128, 128), F32),
             pltpu.VMEM((128, 128), F32),
@@ -404,17 +412,17 @@
             pltpu.VMEM((16, 128), F32),
             pltpu.VMEM((128, 128), F32),
             pltpu.VMEM((128, 128), F32),
-            dma, dma, dma((NZ,)), dma, dma((NZ,)), dma((NZ,)), dma((NZ,)),
+            dma((6,)), dma, dma((NZ,)), dma, dma((NZ,)), dma((NZ,)), dma((NZ,)),
             dma, dma, dma, dma,
             dma, dma((12,)),
             dma, dma, dma,
         ],
         compiler_params=pltpu.CompilerParams(
-            collective_id=0, has_side_effects=True, vmem_limit_bytes=40 * 1024 * 1024
+            collective_id=0, has_side_effects=True, vmem_limit_bytes=60 * 1024 * 1024
         ),
     )(
         embeddings,
-        send_list[0],
+        send_list[0].T,
         send_count,
         parent_id[None, :],
         child_count,

time: 105 us -> 88.2 us (0.84)
  Pallas kernels: 97 us -> 84.5 us
  local copies, waits for them, and re-layouts: 6.77 us -> 2.82 us
    pallas_call x1, Pallas kernels: 97 us -> 84.5 us  [on_device(): pl.pallas_call(kernel, name='refine', out_shape=(jax.ShapeDtypeStruct((PA...]
    unnamed x13 -> x4, local copies, waits for them, and re-layouts: 6.77 us -> 2.82 us
where the time goes in v2:
time: 88.2 us; the launch traced here: 88 us
  Pallas kernels  84.5 us (96%)
  local copies, waits for them, and re-layouts  2.82 us (3%)
    pallas_call x1, Pallas kernels, on_device(): pl.pallas_call(kernel, name='refine', out_shape=(jax.ShapeDtypeStruct((PA...  84.5 us
    unnamed x4, local copies, waits for them, and re-layouts  2.82 us

profile of v2, /device:TPU:1, one launch (start us, length us, event | category | flops | bytes accessed | tf_op | source)
XLA Modules:
  0.0 88.0 jit_solution(6110967432179828095)
XLA Ops:
  0.6 84.5 %refine.1 = (f32[8,32,1024]{2,1,0:T(8,128)}, f32[1,128]{1,0:T(1,128)}) custom-call(bf16[128,1024]{1,0:T(8,128)(2,1)} %emb_hbm.1, s32[2,128]{1,0:T(2,128)} %bitcast.5, s32[1,128]{1,0:T(1,128)} %counting_hbm.1, s32[1,128]{1,0:T(1,128)} %bitcast.6, s32[8]{0:T(128)} %ccount_hbm.1, bf16[8,128,1024]{2,1,0:T(8,128)(2,1)} %cent.1), custom_call_target="tpu_custom_call" | custom-call | tf_op jit(solution)/shard_map/refine/pallas_call | solution.py:378
  85.2 0.0 copy-start
  85.2 2.3 %copy.10 = f32[8,32,1024]{2,1,0:T(8,128)} copy(f32[8,32,1024]{2,1,0:T(8,128)} %get-tuple-element.8) | data formatting | bytes 2097152
  87.5 0.0 copy-done
  87.5 0.5 copy.11
Async XLA Ops:
  85.2 2.3 %copy-start = (f32[1,128]{1,0:T(1,128)S(1)}, f32[1,128]{1,0:T(1,128)}, u32[]{:S(2)}) copy-start(f32[1,128]{1,0:T(1,128)} %get-tuple-element.5) | copy-start | bytes 1540

commit v3 on v2

v3 whole, which is shorter than its diff:
```python
import functools

import jax
import jax.numpy as jnp
from jax import lax
from jax.experimental import pallas as pl
from jax.experimental.pallas import tpu as pltpu
from jax.sharding import PartitionSpec as P

MESH = pl.DeviceIdType.MESH
F32 = jnp.float32
BF16 = jnp.bfloat16

NZ, NG, NQ = 16, 8, 4
NR = NZ * NG
HALF = NZ // 2
PAR, KIDS, SHARE, D = 8, 128, 32, 1024
COLS = PAR * SHARE
FLOOR = -1e30
LEAD, LAG = 8, 3
TEMP = 1.0 / 32.0


def sdz(s):
    odd = lax.rem(s, 2)
    return odd * lax.div(s + 1, 2) + (1 - odd) * (NZ - lax.div(s, 2))


def mult(x, m):
    return pl.multiple_of(x, m)


def iota(shape, dim):
    return lax.broadcasted_iota(jnp.int32, shape, dim)


def kernel(
    emb_hbm, listing_hbm, counting_hbm, parent_hbm, ccount_hbm, cent,
    out, energy,
    emb, listing, counting, parent, ccount,
    stage, tiles, xg, rows_f, xs, full, panel, norms, lg, terms, resp, wsum,
    meta_o, zb, sb, yb, mx, xm, mt,
    sx, rx, sc, est, eb, fs, fb, fo,
    in_sem, zss, zrs, xss, xrl, xrr, xrf, mss, mzr, myr, mxr, sss, srs, ess, ezr, eyr,
):
    r = lax.axis_index("rows")
    q = lax.axis_index("rep")
    z = lax.div(r, NG)
    g = lax.rem(r, NG)
    right = lax.rem(q + 1, NQ)
    left = lax.rem(q + 3, NQ)
    opp = lax.rem(q + 2, NQ)

    def remote(src, dst, ss, rs, dev):
        return pltpu.make_async_remote_copy(
            src_ref=src, dst_ref=dst, send_sem=ss, recv_sem=rs, device_id=dev, device_id_type=MESH
        )

    loads = [
        pltpu.make_async_copy(src, dst, in_sem.at[k])
        for k, (src, dst) in enumerate((
            (emb_hbm, emb),
            (listing_hbm, listing),
            (counting_hbm, counting),
            (parent_hbm, parent),
            (ccount_hbm, ccount),
            (cent.at[:, pl.ds(mult(q * SHARE, SHARE), SHARE), :], panel),
            (cent, full),
        ))
    ]
    for load in loads:
        load.start()

    barrier = pltpu.get_barrier_semaphore()

    @pl.loop(1, NR)
    def _(i):
        pl.semaphore_signal(
            barrier, inc=1, device_id=(lax.rem(r + i, NR), q), device_id_type=MESH
        )

    for peer in (right, left, opp):
        pl.semaphore_signal(barrier, inc=1, device_id=(r, peer), device_id_type=MESH)

    for load in loads:
        load.wait()

    lane = iota((NR, NR), 1)
    row_i = iota((NR, NR), 0)
    count_col = jnp.sum(jnp.where(lane == row_i, counting[...].astype(F32), 0.0), axis=1, keepdims=True)
    par_row = lax.rem(parent[...], PAR).astype(F32)
    listed = []
    for j in range(2):
        wide = jnp.where(lane == row_i, listing[j : j + 1, :].astype(F32), 0.0)
        listed.append(jnp.sum(wide, axis=1, keepdims=True).astype(jnp.int32))
    meta = jnp.zeros((NR, NR), F32)
    for j in range(2):
        hot = (lane == listed[j]) & (count_col > j)
        code = jnp.sum(jnp.where(hot, par_row + 1.0, 0.0), axis=1, keepdims=True)
        meta = meta + jnp.where(lax.rem(lane, 16) == g * 2 + j, code, 0.0)
        picked = jnp.dot(hot.astype(BF16), emb[...], preferred_element_type=F32)
        for k in range(8):
            stage[pl.ds(j * 8 + k, NR, stride=16), :] = picked[:, 128 * k : 128 * (k + 1)]
    tiles[...] = stage[...].astype(BF16)
    meta_o[...] = meta

    kid = iota((KIDS, 1), 0)
    for p in range(PAR):
        wide = full[p].astype(F32)
        norm = jnp.sum(wide * wide, axis=1, keepdims=True) * TEMP
        norms[p * KIDS : (p + 1) * KIDS, :] = jnp.where(kid < ccount[p], norm, -FLOOR)

    pl.semaphore_wait(barrier, NR - 1 + NQ - 1)

    def send_rows(s, i):
        zt = lax.rem(z + sdz(s), NZ)
        o = zt * NG + lax.rem(g + i, NG)
        remote(
            tiles.at[pl.ds(mult(o * 16, 16), 16)],
            xg.at[pl.ds(mult((s * NQ + q) * 128 + g * 16, 16), 16)],
            zss, zrs.at[s], (o, q),
        ).start()

    @pl.loop(1, NG)
    def _(i):
        send_rows(0, i)

    xg[pl.ds(mult(q * 128 + g * 16, 16), 16), :] = tiles[pl.ds(mult(r * 16, 16), 16), :]
    zb[0:8, :] = meta_o[pl.ds(mult(z * 8, 8), 8), :]

    def chunk(t, qq):
        return xg.at[pl.ds(mult((t * NQ + qq) * 128, 128), 128)]

    def step(s):
        @pl.when(s < NZ)
        def _():
            @pl.when(s > 0)
            def _():
                remote(chunk(s, q), chunk(s, q), zss, zrs.at[s], (r, right)).wait_recv()

            @pl.when(s == 0)
            def _():
                part = xg.at[pl.ds(0, 112)]
                remote(part, part, zss, zrs.at[s], (r, right)).wait_recv()

            for rs, peer in ((xrl, right), (xrr, left), (xrf, opp)):
                remote(chunk(s, q), chunk(s, q), xss, rs.at[s], (r, peer)).start()

        @pl.when(s >= LAG)
        def _():
            t = s - LAG
            for rs, peer in ((xrl, left), (xrr, right), (xrf, opp)):
                remote(chunk(t, q), chunk(t, peer), xss, rs.at[t], (r, peer)).wait_recv()
            rows_f[...] = xg[pl.ds(mult(t * 512, 512), 512), :].astype(F32)
            for k in range(8):
                xs[pl.ds(mult(t * 64, 64), 64), 128 * k : 128 * (k + 1)] = rows_f[
                    pl.ds(k, 64, stride=8), :
                ].astype(BF16)

    def send_steps(first, last):
        @pl.loop(first, last)
        def _(s):
            @pl.loop(0, NG)
            def _(i):
                send_rows(s, i)

            @pl.when(s >= LEAD)
            def _():
                step(s - LEAD)

    send_steps(1, 5)

    @pl.loop(1, NZ)
    def _(k):
        s = NZ - k
        zt = lax.rem(z + sdz(s), NZ)
        remote(
            meta_o.at[pl.ds(mult(zt * NG, 8), 8)], zb.at[pl.ds(mult(s * 8, 8), 8)],
            mss, mzr, (zt * NG + g, q),
        ).start()

    send_steps(5, NZ)

    mate = meta_o.at[pl.ds(0, 120)]
    remote(mate, zb.at[pl.ds(0, 120)], mss, mzr, (r, right)).wait_recv()
    for gg in range(NG):
        sb[gg * 16 : (gg + 1) * 16, :] = zb[pl.ds(gg, 16, stride=8), :]

    @pl.loop(1, NG)
    def _(i):
        gt = lax.rem(g + i, NG)
        remote(
            sb.at[pl.ds(mult(gt * 16, 16), 16)], yb.at[pl.ds(mult(g * 16, 16), 16)],
            mss, myr, (z * NG + gt, q),
        ).start()

    yb[pl.ds(mult(g * 16, 16), 16), :] = sb[pl.ds(mult(g * 16, 16), 16), :]

    pl.loop(NZ - LEAD, NZ - LEAD + 1)(step)

    mate = sb.at[pl.ds(0, 112)]
    remote(mate, yb.at[pl.ds(0, 112)], mss, myr, (r, right)).wait_recv()
    slot = yb[0:16, :]
    for gg in range(1, NG):
        slot = slot + yb[gg * 16 : (gg + 1) * 16, :]
    sl = iota((16, 128), 0)
    ln = iota((16, 128), 1)
    mine = lax.rem(lax.div(ln, 16), NQ) == q
    for b in range(8):
        here = mine & (sl == 2 * b + lax.div(ln, 64))
        mx[b : b + 1, :] = jnp.sum(jnp.where(here, slot, 0.0), axis=0, keepdims=True)
    for k, peer in enumerate((right, left, opp)):
        remote(mx, xm.at[pl.ds(mult(q * 8, 8), 8)], mss, mxr, (r, peer)).start()
    xm[pl.ds(mult(q * 8, 8), 8), :] = mx[...]

    pl.loop(NZ - LEAD + 1, NZ - LEAD + 3)(step)

    mate = xm.at[pl.ds(0, 24)]
    remote(mate, mate, mss, mxr, (r, right)).wait_recv()

    mt[...] = xm[0:8, :] + xm[8:16, :] + xm[16:24, :] + xm[24:32, :]
    wsum[...] = jnp.zeros((COLS, 128), F32)

    def codes(b0, nb):
        return jnp.concatenate([mt[b : b + 1, :] for b in range(b0, b0 + nb)], axis=1)

    def gather_logits(code, kids, lanes):
        logits = jnp.full((kids, lanes), FLOOR, F32)
        for p in range(PAR):
            rows = slice(p * kids, (p + 1) * kids)
            value = lg[rows, 0:lanes] * (2.0 * TEMP) - norms[rows, :]
            logits = jnp.where(code == p + 1.0, value, logits)
        return logits

    def spread(code, b0, nb, share):
        for p in range(PAR):
            rows = slice(p * SHARE, (p + 1) * SHARE)
            value = jnp.where(code == p + 1.0, share, 0.0)
            resp[rows, b0 * 128 : (b0 + nb) * 128] = value.astype(BF16)
            total = value[:, 0:128]
            for b in range(1, nb):
                total = total + value[:, b * 128 : (b + 1) * 128]
            wsum[rows, :] = wsum[rows, :] + total

    def first_pass(b0, nb):
        lanes = nb * 128
        code = codes(b0, nb)
        lg[:, 0:lanes] = lax.dot_general(
            full[...].reshape(PAR * KIDS, D), xs[b0 * 128 : b0 * 128 + lanes, :],
            (((1,), (1,)), ((), ())), preferred_element_type=F32,
        )
        logits = gather_logits(code, KIDS, lanes)
        value = jnp.exp(logits - jnp.max(logits, axis=0, keepdims=True))
        total = jnp.sum(value, axis=0, keepdims=True)
        scale = jnp.where(code > 0.5, 1.0 / total, 0.0)
        terms[...] = value
        spread(code, b0, nb, terms[pl.ds(mult(q * SHARE, SHARE), SHARE), :] * scale)

    def update(last):
        inverse = 1.0 / (jnp.sum(wsum[...], axis=1, keepdims=True) + 1.0)
        square = jnp.zeros((COLS, 1), F32)
        for b in range(4):
            cols = slice(b * 256, (b + 1) * 256)
            sums = jnp.dot(resp[...], xs[:, cols], preferred_element_type=F32)
            old = panel[:, :, cols].reshape(COLS, 256).astype(F32)
            new = (sums + old) * inverse
            if last:
                out[:, :, cols] = new.reshape(PAR, SHARE, 256)
            else:
                low = new.astype(BF16)
                panel[:, :, cols] = low.reshape(PAR, SHARE, 256)
                wide = low.astype(F32)
                square = square + jnp.sum(wide * wide, axis=1, keepdims=True)
        return square

    first_pass(0, 2)
    pl.loop(NZ - 5, NZ - 4)(step)
    first_pass(2, 2)
    pl.loop(NZ - 4, NZ)(step)
    first_pass(4, 2)
    pl.loop(NZ, NZ + LAG)(step)
    first_pass(6, 2)
    square = update(False)

    kid = iota((SHARE, 1), 0) + q * SHARE
    for p in range(PAR):
        rows = slice(p * SHARE, (p + 1) * SHARE)
        norms[rows, :] = jnp.where(kid < ccount[p], square[rows] * TEMP, -FLOOR)
    wsum[...] = jnp.zeros((COLS, 128), F32)
    for h in range(4):
        code = codes(h * 2, 2)
        lg[0:COLS, 0:256] = lax.dot_general(
            panel[...].reshape(COLS, D), xs[h * 256 : (h + 1) * 256, :],
            (((1,), (1,)), ((), ())), preferred_element_type=F32,
        )
        logits = gather_logits(code, SHARE, 256)
        top = jnp.max(logits, axis=0, keepdims=True)
        value = jnp.exp(logits - top)
        total = jnp.sum(value, axis=0, keepdims=True)
        terms[h * SHARE : (h + 1) * SHARE, :] = value
        for b in range(2):
            sx[h * 2 + b : h * 2 + b + 1, :] = top[:, b * 128 : (b + 1) * 128]
            sx[8 + h * 2 + b : 9 + h * 2 + b, :] = total[:, b * 128 : (b + 1) * 128]
    peers = (right, left, opp)
    for k, peer in enumerate(peers):
        remote(sx, rx.at[pl.ds(k * 16, 16)], sss, srs.at[k], (r, peer)).start()
    tops, totals = [sx[0:8, :]], [sx[8:16, :]]
    for k in range(3):
        remote(sx, rx.at[pl.ds(k * 16, 16)], sss, srs.at[k], (r, right)).wait_recv()
        tops.append(rx[k * 16 : k * 16 + 8, :])
        totals.append(rx[k * 16 + 8 : k * 16 + 16, :])
    top = jnp.maximum(jnp.maximum(tops[0], tops[1]), jnp.maximum(tops[2], tops[3]))
    own = jnp.exp(tops[0] - top)
    total = totals[0] * own
    for k in range(1, 4):
        total = total + totals[k] * jnp.exp(tops[k] - top)
    est[...] = top + jnp.log(total)

    @pl.loop(1, NZ)
    def _(k):
        s = NZ - k
        zt = lax.rem(z + NZ - sdz(s), NZ)
        remote(est, eb.at[z], ess, ezr, (zt * NG + g, q)).start()

    sc[...] = jnp.where(mt[...] > 0.5, own / total, 0.0)
    for h in range(4):
        scale = jnp.concatenate([sc[h * 2 : h * 2 + 1, :], sc[h * 2 + 1 : h * 2 + 2, :]], axis=1)
        spread(codes(h * 2, 2), h * 2, 2, terms[h * SHARE : (h + 1) * SHARE, :] * scale)
    update(True)

    def step_of(dz):
        return jnp.where((dz >= 1) & (dz <= HALF), 2 * dz - 1, lax.rem(2 * (NZ - dz), 2 * NZ))

    mate = eb.at[pl.ds(0, NZ - 1)]
    remote(mate, mate, ess, ezr, (r, right)).wait_recv()
    eb[z] = est[...]
    shape = (NZ, 8, 128)
    block = lax.div(step_of(lax.rem(iota(shape, 0) + NZ - z, NZ)), 2)
    fs[...] = jnp.sum(jnp.where(iota(shape, 1) == block, eb[...], 0.0), axis=1)

    @pl.loop(1, NG)
    def _(i):
        gt = lax.rem(g + i, NG)
        remote(fs, fb.at[pl.ds(mult(g * 16, 16), 16)], ess, eyr, (z * NG + gt, q)).start()

    mate = fb.at[pl.ds(0, 112)]
    remote(mate, mate, ess, eyr, (r, right)).wait_recv()
    fb[pl.ds(mult(g * 16, 16), 16), :] = fs[...]
    for gg in range(NG):
        fo[pl.ds(gg, 16, stride=8), :] = fb[gg * 16 : (gg + 1) * 16, :]
    dz = lax.rem(lax.div(row_i, NG) + NZ - z, NZ)
    at = lax.rem(step_of(dz), 2) * 64 + q * 16 + g * 2
    home = jnp.zeros((1, NR), F32)
    for j in range(2):
        hot = (lane == listed[j]) & (count_col > j)
        value = jnp.sum(jnp.where(lane == at + j, fo[...], 0.0), axis=1, keepdims=True)
        home = home + jnp.sum(jnp.where(hot, value, 0.0), axis=0, keepdims=True)
    energy[...] = home

    def drain(ref, sem):
        remote(ref, ref, sem, eyr, (r, right)).wait_send()

    drain(tiles.at[pl.ds(0, 127 * 16)], zss)
    drain(xg.at[pl.ds(0, 48 * 128)], xss)
    drain(stage.at[pl.ds(0, 256)], mss)
    drain(rx, sss)
    drain(stage.at[pl.ds(0, 232)], ess)


def on_device(embeddings, parent_id, send_list, send_count, child_count, centroids):
    dma = pltpu.SemaphoreType.DMA
    vmem = pl.BlockSpec(memory_space=pltpu.VMEM)
    updated, row_energy = pl.pallas_call(
        kernel,
        name="refine",
        out_shape=(
            jax.ShapeDtypeStruct((PAR, SHARE, D), F32),
            jax.ShapeDtypeStruct((1, NR), F32),
        ),
        in_specs=[pl.BlockSpec(memory_space=pltpu.HBM)] * 6,
        out_specs=(vmem, vmem),
        scratch_shapes=[
            pltpu.VMEM((NR, D), BF16),
            pltpu.VMEM((2, NR), jnp.int32),
            pltpu.VMEM((1, NR), jnp.int32),
            pltpu.VMEM((1, NR), jnp.int32),
            pltpu.SMEM((PAR,), jnp.int32),
            pltpu.VMEM((2048, 128), F32),
            pltpu.VMEM((2048, 128), BF16),
            pltpu.VMEM((64 * 128, 128), BF16),
            pltpu.VMEM((512, 128), F32),
            pltpu.VMEM((1024, D), BF16),
            pltpu.VMEM((PAR, KIDS, D), BF16),
            pltpu.VMEM((PAR, SHARE, D), BF16),
            pltpu.VMEM((PAR * KIDS, 1), F32),
            pltpu.VMEM((PAR * KIDS, 256), F32),
            pltpu.VMEM((KIDS, 256), F32),
            pltpu.VMEM((COLS, 1024), BF16),
            pltpu.VMEM((COLS, 128), F32),
            pltpu.VMEM((128, 128), F32),
            pltpu.VMEM((128, 128), F32),
            pltpu.VMEM((128, 128), F32),
            pltpu.VMEM((128, 128), F32),
            pltpu.VMEM((8, 128), F32),
            pltpu.VMEM((32, 128), F32),
            pltpu.VMEM((8, 128), F32),
            pltpu.VMEM((16, 128), F32),
            pltpu.VMEM((48, 128), F32),
            pltpu.VMEM((8, 128), F32),
            pltpu.VMEM((8, 128), F32),
            pltpu.VMEM((NZ, 8, 128), F32),
            pltpu.VMEM((16, 128), F32),
            pltpu.VMEM((128, 128), F32),
            pltpu.VMEM((128, 128), F32),
            dma((7,)), dma, dma((NZ,)), dma, dma((NZ,)), dma((NZ,)), dma((NZ,)),
            dma, dma, dma, dma,
            dma, dma((3,)),
            dma, dma, dma,
        ],
        compiler_params=pltpu.CompilerParams(
            collective_id=0, has_side_effects=True, vmem_limit_bytes=60 * 1024 * 1024
        ),
    )(
        embeddings,
        send_list[0].T,
        send_count,
        parent_id[None, :],
        child_count,
        centroids,
    )
    return (updated, row_energy[0])


def solution(mesh):
    in_specs = (
        P(("rows", "rep"), None),
        P(("rows", "rep")),
        P(("rows", "rep"), None, None),
        P(("rows", "rep"), None),
        P("rows"),
        P("rows", None, None),
    )
    out_specs = (P("rows", "rep", None), P(("rows", "rep")))
    return jax.shard_map(
        on_device, mesh=mesh, in_specs=in_specs, out_specs=out_specs, check_vma=False
    )
```

time: 88.2 us -> 78.9 us (0.89)
  Pallas kernels: 84.5 us -> 75.3 us
    pallas_call x1, Pallas kernels: 84.5 us -> 75.3 us  [on_device(): pl.pallas_call(kernel, name='refine', out_shape=(jax.ShapeDtypeStruct((PA...]
where the time goes in v3:
time: 78.9 us; the launch traced here: 78.8 us
  Pallas kernels  75.3 us (95%)
  local copies, waits for them, and re-layouts  2.82 us (4%)
    pallas_call x1, Pallas kernels, on_device(): pl.pallas_call(kernel, name='refine', out_shape=(jax.ShapeDtypeStruct((PA...  75.3 us
    unnamed x4, local copies, waits for them, and re-layouts  2.82 us

profile of v3, /device:TPU:1, one launch (start us, length us, event | category | flops | bytes accessed | tf_op | source)
XLA Modules:
  0.0 78.8 jit_solution(16632453789387437400)
XLA Ops:
  0.6 75.3 %refine.1 = (f32[8,32,1024]{2,1,0:T(8,128)}, f32[1,128]{1,0:T(1,128)}) custom-call(bf16[128,1024]{1,0:T(8,128)(2,1)} %emb_hbm.1, s32[2,128]{1,0:T(2,128)} %bitcast.5, s32[1,128]{1,0:T(1,128)} %counting_hbm.1, s32[1,128]{1,0:T(1,128)} %bitcast.6, s32[8]{0:T(128)} %ccount_hbm.1, bf16[8,128,1024]{2,1,0:T(8,128)(2,1)} %cent.1), custom_call_target="tpu_custom_call" | custom-call | tf_op jit(solution)/shard_map/refine/pallas_call | solution.py:373
  75.9 0.0 copy-start
  75.9 2.3 %copy.10 = f32[8,32,1024]{2,1,0:T(8,128)} copy(f32[8,32,1024]{2,1,0:T(8,128)} %get-tuple-element.8) | data formatting | bytes 2097152
  78.3 0.0 copy-done
  78.3 0.5 copy.11
Async XLA Ops:
  75.9 2.3 %copy-start = (f32[1,128]{1,0:T(1,128)S(1)}, f32[1,128]{1,0:T(1,128)}, u32[]{:S(2)}) copy-start(f32[1,128]{1,0:T(1,128)} %get-tuple-element.5) | copy-start | bytes 1540

commit v4 on v3

--- a/solution.py
+++ b/solution.py
@@ -41,7 +41,7 @@
     stage, tiles, xg, rows_f, xs, full, panel, norms, lg, terms, resp, wsum,
     meta_o, zb, sb, yb, mx, xm, mt,
     sx, rx, sc, est, eb, fs, fb, fo,
-    in_sem, zss, zrs, xss, xrl, xrr, xrf, mss, mzr, myr, mxr, sss, srs, ess, ezr, eyr,
+    up_sem, down_sem, in_sem, zss, zrs, xss, xrl, xrr, xrf, mss, mzr, myr, mxr, sss, srs, ess, ezr, eyr,
 ):
     r = lax.axis_index("rows")
     q = lax.axis_index("rep")
@@ -72,15 +72,15 @@
         load.start()
 
     barrier = pltpu.get_barrier_semaphore()
-
-    @pl.loop(1, NR)
+    up = (lax.rem(z + 1, NZ) * NG + g, q)
+    down = (lax.rem(z + NZ - 1, NZ) * NG + g, q)
+    for peer in (up, down, (r, right), (r, left), (r, opp)):
+        pl.semaphore_signal(barrier, inc=1, device_id=peer, device_id_type=MESH)
+
+    @pl.loop(1, NG)
     def _(i):
-        pl.semaphore_signal(
-            barrier, inc=1, device_id=(lax.rem(r + i, NR), q), device_id_type=MESH
-        )
-
-    for peer in (right, left, opp):
-        pl.semaphore_signal(barrier, inc=1, device_id=(r, peer), device_id_type=MESH)
+        mate = z * NG + lax.rem(g + i, NG)
+        pl.semaphore_signal(barrier, inc=1, device_id=(mate, q), device_id_type=MESH)
 
     for load in loads:
         load.wait()
@@ -110,7 +110,10 @@
         norm = jnp.sum(wide * wide, axis=1, keepdims=True) * TEMP
         norms[p * KIDS : (p + 1) * KIDS, :] = jnp.where(kid < ccount[p], norm, -FLOOR)
 
-    pl.semaphore_wait(barrier, NR - 1 + NQ - 1)
+    pl.semaphore_wait(barrier, 2 + NQ - 1 + NG - 1)
+
+    pl.semaphore_signal(up_sem, inc=1, device_id=down, device_id_type=MESH)
+    pl.semaphore_signal(down_sem, inc=1, device_id=up, device_id_type=MESH)
 
     def send_rows(s, i):
         zt = lax.rem(z + sdz(s), NZ)
@@ -168,18 +171,33 @@
             def _():
                 step(s - LEAD)
 
-    send_steps(1, 5)
-
-    @pl.loop(1, NZ)
-    def _(k):
-        s = NZ - k
+    def send_parents(s):
         zt = lax.rem(z + sdz(s), NZ)
         remote(
             meta_o.at[pl.ds(mult(zt * NG, 8), 8)], zb.at[pl.ds(mult(s * 8, 8), 8)],
             mss, mzr, (zt * NG + g, q),
         ).start()
 
-    send_steps(5, NZ)
+    @pl.loop(1, HALF)
+    def _(d):
+        pl.semaphore_wait(up_sem, 1)
+        pl.semaphore_signal(up_sem, inc=1, device_id=down, device_id_type=MESH)
+        pl.semaphore_wait(down_sem, 1)
+
+        @pl.when(d < HALF - 1)
+        def _():
+            pl.semaphore_signal(down_sem, inc=1, device_id=up, device_id_type=MESH)
+
+        send_parents(2 * d - 1)
+        send_parents(2 * d)
+
+        @pl.loop(0, NG)
+        def _(i):
+            send_rows(d, i)
+
+    pl.semaphore_wait(up_sem, 1)
+    send_parents(NZ - 1)
+    send_steps(HALF, NZ)
 
     mate = meta_o.at[pl.ds(0, 120)]
     remote(mate, zb.at[pl.ds(0, 120)], mss, mzr, (r, right)).wait_recv()
@@ -412,6 +430,7 @@
             pltpu.VMEM((16, 128), F32),
             pltpu.VMEM((128, 128), F32),
             pltpu.VMEM((128, 128), F32),
+            pltpu.SemaphoreType.REGULAR, pltpu.SemaphoreType.REGULAR,
             dma((7,)), dma, dma((NZ,)), dma, dma((NZ,)), dma((NZ,)), dma((NZ,)),
             dma, dma, dma, dma,
             dma, dma((3,)),

time: 78.9 us -> 75.8 us (0.961)
  Pallas kernels: 75.3 us -> 72.1 us
    pallas_call x1, Pallas kernels: 75.3 us -> 72.1 us  [on_device(): pl.pallas_call(kernel, name='refine', out_shape=(jax.ShapeDtypeStruct((PA...]
where the time goes in v4:
time: 75.8 us; the launch traced here: 75.6 us
  Pallas kernels  72.1 us (95%)
  local copies, waits for them, and re-layouts  2.82 us (4%)
    pallas_call x1, Pallas kernels, on_device(): pl.pallas_call(kernel, name='refine', out_shape=(jax.ShapeDtypeStruct((PA...  72.1 us
    unnamed x4, local copies, waits for them, and re-layouts  2.82 us

profile of v4, /device:TPU:1, one launch (start us, length us, event | category | flops | bytes accessed | tf_op | source)
XLA Modules:
  0.0 75.6 jit_solution(6539117963189788578)
XLA Ops:
  0.6 72.1 %refine.1 = (f32[8,32,1024]{2,1,0:T(8,128)}, f32[1,128]{1,0:T(1,128)}) custom-call(bf16[128,1024]{1,0:T(8,128)(2,1)} %emb_hbm.1, s32[2,128]{1,0:T(2,128)} %bitcast.5, s32[1,128]{1,0:T(1,128)} %counting_hbm.1, s32[1,128]{1,0:T(1,128)} %bitcast.6, s32[8]{0:T(128)} %ccount_hbm.1, bf16[8,128,1024]{2,1,0:T(8,128)(2,1)} %cent.1), custom_call_target="tpu_custom_call" | custom-call | tf_op jit(solution)/shard_map/refine/pallas_call | solution.py:391
  72.7 0.0 copy-start
  72.8 2.3 %copy.10 = f32[8,32,1024]{2,1,0:T(8,128)} copy(f32[8,32,1024]{2,1,0:T(8,128)} %get-tuple-element.8) | data formatting | bytes 2097152
  75.1 0.0 copy-done
  75.1 0.5 copy.11
Async XLA Ops:
  72.7 2.3 %copy-start = (f32[1,128]{1,0:T(1,128)S(1)}, f32[1,128]{1,0:T(1,128)}, u32[]{:S(2)}) copy-start(f32[1,128]{1,0:T(1,128)} %get-tuple-element.5) | copy-start | bytes 1540

commit v5 on v4

--- a/solution.py
+++ b/solution.py
@@ -1,5 +1,3 @@
-import functools
-
 import jax
 import jax.numpy as jnp
 from jax import lax
@@ -36,8 +34,8 @@
 
 def kernel(
     emb_hbm, listing_hbm, counting_hbm, parent_hbm, ccount_hbm, cent,
-    out, energy,
-    emb, listing, counting, parent, ccount,
+    out_hbm, energy,
+    out, out_sem, emb, listing, counting, parent, ccount,
     stage, tiles, xg, rows_f, xs, full, panel, norms, lg, terms, resp, wsum,
     meta_o, zb, sb, yb, mx, xm, mt,
     sx, rx, sc, est, eb, fs, fb, fo,
@@ -82,7 +80,7 @@
         mate = z * NG + lax.rem(g + i, NG)
         pl.semaphore_signal(barrier, inc=1, device_id=(mate, q), device_id_type=MESH)
 
-    for load in loads:
+    for load in loads[:4]:
         load.wait()
 
     lane = iota((NR, NR), 1)
@@ -104,12 +102,6 @@
     tiles[...] = stage[...].astype(BF16)
     meta_o[...] = meta
 
-    kid = iota((KIDS, 1), 0)
-    for p in range(PAR):
-        wide = full[p].astype(F32)
-        norm = jnp.sum(wide * wide, axis=1, keepdims=True) * TEMP
-        norms[p * KIDS : (p + 1) * KIDS, :] = jnp.where(kid < ccount[p], norm, -FLOOR)
-
     pl.semaphore_wait(barrier, 2 + NQ - 1 + NG - 1)
 
     pl.semaphore_signal(up_sem, inc=1, device_id=down, device_id_type=MESH)
@@ -163,8 +155,7 @@
     def send_steps(first, last):
         @pl.loop(first, last)
         def _(s):
-            @pl.loop(0, NG)
-            def _(i):
+            for i in range(NG):
                 send_rows(s, i)
 
             @pl.when(s >= LEAD)
@@ -191,13 +182,21 @@
         send_parents(2 * d - 1)
         send_parents(2 * d)
 
-        @pl.loop(0, NG)
-        def _(i):
+        for i in range(NG):
             send_rows(d, i)
 
     pl.semaphore_wait(up_sem, 1)
     send_parents(NZ - 1)
     send_steps(HALF, NZ)
+
+    for load in loads[4:]:
+        load.wait()
+
+    kid = iota((KIDS, 1), 0)
+    for p in range(PAR):
+        wide = full[p].astype(F32)
+        norm = jnp.sum(wide * wide, axis=1, keepdims=True) * TEMP
+        norms[p * KIDS : (p + 1) * KIDS, :] = jnp.where(kid < ccount[p], norm, -FLOOR)
 
     mate = meta_o.at[pl.ds(0, 120)]
     remote(mate, zb.at[pl.ds(0, 120)], mss, mzr, (r, right)).wait_recv()
@@ -214,7 +213,7 @@
 
     yb[pl.ds(mult(g * 16, 16), 16), :] = sb[pl.ds(mult(g * 16, 16), 16), :]
 
-    pl.loop(NZ - LEAD, NZ - LEAD + 1)(step)
+    pl.loop(NZ - LEAD, 10)(step)
 
     mate = sb.at[pl.ds(0, 112)]
     remote(mate, yb.at[pl.ds(0, 112)], mss, myr, (r, right)).wait_recv()
@@ -231,7 +230,8 @@
         remote(mx, xm.at[pl.ds(mult(q * 8, 8), 8)], mss, mxr, (r, peer)).start()
     xm[pl.ds(mult(q * 8, 8), 8), :] = mx[...]
 
-    pl.loop(NZ - LEAD + 1, NZ - LEAD + 3)(step)
+    pl.loop(10, 12)(step)
+    pl.loop(12, NZ)(step)
 
     mate = xm.at[pl.ds(0, 24)]
     remote(mate, mate, mss, mxr, (r, right)).wait_recv()
@@ -292,9 +292,7 @@
         return square
 
     first_pass(0, 2)
-    pl.loop(NZ - 5, NZ - 4)(step)
     first_pass(2, 2)
-    pl.loop(NZ - 4, NZ)(step)
     first_pass(4, 2)
     pl.loop(NZ, NZ + LAG)(step)
     first_pass(6, 2)
@@ -345,6 +343,8 @@
         scale = jnp.concatenate([sc[h * 2 : h * 2 + 1, :], sc[h * 2 + 1 : h * 2 + 2, :]], axis=1)
         spread(codes(h * 2, 2), h * 2, 2, terms[h * SHARE : (h + 1) * SHARE, :] * scale)
     update(True)
+    store = pltpu.make_async_copy(out, out_hbm, out_sem)
+    store.start()
 
     def step_of(dz):
         return jnp.where((dz >= 1) & (dz <= HALF), 2 * dz - 1, lax.rem(2 * (NZ - dz), 2 * NZ))
@@ -375,6 +375,8 @@
         home = home + jnp.sum(jnp.where(hot, value, 0.0), axis=0, keepdims=True)
     energy[...] = home
 
+    store.wait()
+
     def drain(ref, sem):
         remote(ref, ref, sem, eyr, (r, right)).wait_send()
 
@@ -396,8 +398,10 @@
             jax.ShapeDtypeStruct((1, NR), F32),
         ),
         in_specs=[pl.BlockSpec(memory_space=pltpu.HBM)] * 6,
-        out_specs=(vmem, vmem),
+        out_specs=(pl.BlockSpec(memory_space=pltpu.HBM), vmem),
         scratch_shapes=[
+            pltpu.VMEM((PAR, SHARE, D), F32),
+            dma,
             pltpu.VMEM((NR, D), BF16),
             pltpu.VMEM((2, NR), jnp.int32),
             pltpu.VMEM((1, NR), jnp.int32),

time: 75.8 us -> 75.1 us (level)
  no operation moved by 1% of the time
where the time goes in v5:
time: 75.1 us; the launch traced here: 75 us
  Pallas kernels  71.5 us (95%)
  local copies, waits for them, and re-layouts  2.82 us (4%)
    pallas_call x1, Pallas kernels, on_device(): pl.pallas_call(kernel, name='refine', out_shape=(jax.ShapeDtypeStruct((PA...  71.5 us
    unnamed x4, local copies, waits for them, and re-layouts  2.82 us

profile of v5, /device:TPU:1, one launch (start us, length us, event | category | flops | bytes accessed | tf_op | source)
XLA Modules:
  0.0 75.0 jit_solution(167554261080829375)
XLA Ops:
  0.6 71.5 %refine.1 = (f32[8,32,1024]{2,1,0:T(8,128)}, f32[1,128]{1,0:T(1,128)}) custom-call(bf16[128,1024]{1,0:T(8,128)(2,1)} %emb_hbm.1, s32[2,128]{1,0:T(2,128)} %bitcast.5, s32[1,128]{1,0:T(1,128)} %counting_hbm.1, s32[1,128]{1,0:T(1,128)} %bitcast.6, s32[8]{0:T(128)} %ccount_hbm.1, bf16[8,128,1024]{2,1,0:T(8,128)(2,1)} %cent.1), custom_call_target="tpu_custom_call" | custom-call | tf_op jit(solution)/shard_map/refine/pallas_call | solution.py:393
  72.1 0.0 copy-start
  72.2 2.3 %copy.10 = f32[8,32,1024]{2,1,0:T(8,128)} copy(f32[8,32,1024]{2,1,0:T(8,128)} %get-tuple-element.8) | data formatting | bytes 2097152
  74.5 0.0 copy-done
  74.5 0.5 copy.11
Async XLA Ops:
  72.1 2.3 %copy-start = (f32[1,128]{1,0:T(1,128)S(1)}, f32[1,128]{1,0:T(1,128)}, u32[]{:S(2)}) copy-start(f32[1,128]{1,0:T(1,128)} %get-tuple-element.5) | copy-start | bytes 1540
